TPU v7x, 32 devices: a whole 2x2x4 slice. The times are simulated.
32 devices in a mesh: ens: 2 (over y), lon: 4 (over z), lat: 4 (over x, core).
Axes of the slice: x: 2, y: 2, z: 4, core: 2. Of those that a mesh axis runs over, the one named last changes fastest.
Arguments:
- state: float32 [32, 512, 512], P('ens', 'lat', 'lon'), parts along dimension 0, may hold values from -6 to 6
- cotangent: float32 [32, 512, 512], P('ens', 'lat', 'lon'), parts along dimension 0, may hold values from -8 to 8
- land_mask: int32 [512, 512], P('lat', 'lon'), may hold values from 0 to 1, as said below
- level_count: int32 [512, 512], P('lat', 'lon'), may hold values from 1 to 16
- fold_partner: int32 [512], P('lon'), may hold values from 0 to 511, as said below
- weight_in: bfloat16 [32, 256], replicated, may hold values from -1 to 1
- weight_out: bfloat16 [256, 16], replicated, may hold values from -0.375 to 0.375
- bias_hidden: float32 [256], replicated, may hold values from -3 to 3
Outputs:
- adjoint_in: float32 [32, 512, 512], P('ens', 'lat', 'lon'), parts along dimension 0
- grad_in: float32 [64, 256], P('ens'), parts along dimension 0
- grad_out: float32 [512, 16], P('ens'), parts along dimension 0
- grad_bias: float32 [512], P('ens'), parts along dimension 0
There are 2 independent parts, one for each index of `ens`. A program takes and returns all parts, laid end to end along the dimension named above; an argument that names none is the same for every part. Nothing has to cross between parts.
Inputs may be any that keep to these rules, and one draw needn't show every extreme that they name: fold_partner[i] = (c - i) modulo 512 for one even whole number c, so fold_partner[fold_partner[i]] = i. `land_mask`: the top two rows are all ocean.
All inputs are finite; a program needn't handle non-finite values.
Results may differ from a plain program's by a relative error of at most 0.0029.
Values sent between devices are 32-bit elements; how exact they have to be, the bound alone decides.
A program may use at most 64 MiB of HBM per device.

v0:
```python
import math

import jax
import jax.numpy as jnp
from jax import lax
from jax.sharding import PartitionSpec as P

L = 16
H = 256
ITERS = 3


DIFFUSE = 0.2
CLOSURE_STEP = 0.5


def with_halo(block, sides, width, periodic):
    for axis, dim in sides:
        count = lax.axis_size(axis)
        forward = [(i, i + 1) for i in range(count - 1)]
        if periodic:
            forward.append((count - 1, 0))
        backward = [(target, source) for source, target in forward]
        low = lax.ppermute(
            lax.slice_in_dim(block, block.shape[dim] - width, None, axis=dim), axis, forward
        )
        high = lax.ppermute(lax.slice_in_dim(block, 0, width, axis=dim), axis, backward)
        block = jnp.concatenate([low, block, high], axis=dim)
    return block


def neighbours(grid_field, fold_partner):
    lon_padded = with_halo(grid_field, (("lon", 2),), 1, True)
    lat_padded = with_halo(grid_field, (("lat", 1),), 1, False)
    top_row = lax.all_gather(grid_field[:, -1, :], "lon", axis=1, tiled=True)
    folded = jnp.take(top_row, fold_partner, axis=1)
    at_top = lax.axis_index("lat") == lax.axis_size("lat") - 1
    north_rim = jnp.where(at_top, folded, lat_padded[:, -1, :])
    north_side = jnp.concatenate([lat_padded[:, 2:-1, :], north_rim[:, None, :]], axis=1)
    return (lon_padded[:, :, 2:], lon_padded[:, :, :-2], north_side, lat_padded[:, :-2, :])


def combine(grid_field, sides, weights):
    total = weights[0] * (sides[0] - grid_field) + weights[1] * (sides[1] - grid_field)
    total = total + weights[2] * (sides[2] - grid_field)
    return total + weights[3] * (sides[3] - grid_field)


def laplace(grid_field, weights, fold_partner):
    return combine(grid_field, neighbours(grid_field, fold_partner), weights)


def squares(residual):
    return lax.psum(jnp.sum(residual * residual), ("lon", "lat"))


def closure_backward(features, closure_grad, weight_in, weight_out, bias_hidden):
    col_count = features.shape[2]
    block_count = features.shape[1] // 8

    def one_block(carry, index):
        feature_grad, grad_in, grad_out, grad_bias = carry
        start = index * 8
        feat_block = lax.dynamic_slice_in_dim(features, start, 8, 1).reshape(2 * L, 8 * col_count)
        grad_block = lax.dynamic_slice_in_dim(closure_grad, start, 8, 1).reshape(L, 8 * col_count)
        pre_act = (
            jnp.einsum("kh,kn->hn", weight_in, feat_block, preferred_element_type=jnp.float32)
            + bias_hidden[:, None]
        )
        activation = jnp.tanh(pre_act)
        act_half = activation.astype(jnp.bfloat16)
        back_act = jnp.einsum(
            "hl,ln->hn", weight_out, grad_block, preferred_element_type=jnp.float32
        )
        back_pre = back_act * (1.0 - activation * activation)
        back_half = back_pre.astype(jnp.bfloat16)
        grad_out = grad_out + jnp.einsum(
            "hn,ln->hl", act_half, grad_block, preferred_element_type=jnp.float32
        )
        grad_in = grad_in + jnp.einsum(
            "kn,hn->kh", feat_block, back_half, preferred_element_type=jnp.float32
        )
        grad_bias = grad_bias + jnp.sum(back_pre, axis=1)
        block_grad = jnp.einsum(
            "kh,hn->kn", weight_in, back_half, preferred_element_type=jnp.float32
        )
        block_grad = block_grad.reshape(2 * L, 8, col_count)
        feature_grad = lax.dynamic_update_slice_in_dim(feature_grad, block_grad, start, 1)
        return ((feature_grad, grad_in, grad_out, grad_bias), None)

    start_carry = (
        jnp.zeros(features.shape, jnp.float32),
        jnp.zeros((2 * L, H), jnp.float32),
        jnp.zeros((H, L), jnp.float32),
        jnp.zeros((H,), jnp.float32),
    )
    carry, _ = lax.scan(one_block, start_carry, jnp.arange(block_count, dtype=jnp.int32))
    return carry


def on_device(
    state, cotangent, land_mask, level_count, fold_partner, weight_in, weight_out, bias_hidden
):
    row_count = state.shape[1]
    col_count = state.shape[2]
    mask_float = land_mask.astype(jnp.float32)
    stacked = jnp.concatenate([state, mask_float[None]], axis=0)
    sides = neighbours(stacked, fold_partner)
    weights = tuple((mask_float * side[L] for side in sides))
    state_lap = combine(state, tuple((side[:L] for side in sides)), weights)
    level_ids = jnp.arange(L, dtype=jnp.int32)[:, None, None]
    live_cells = (
        jnp.where(level_ids < level_count[None], 1.0, 0.0).astype(jnp.float32) * mask_float[None]
    )
    diagonal = 0.1 + 0.3 * jnp.sum(live_cells, axis=0) / L
    inv_root = 1.0 / math.sqrt(L)
    right_side = (-inv_root * jnp.sum(live_cells * cotangent, axis=0))[None]
    pressure = jnp.zeros_like(right_side)
    residual = right_side
    direction = right_side
    norm_now = squares(residual)
    for iteration in range(ITERS):
        image = diagonal * direction - laplace(direction, weights, fold_partner)
        alpha = norm_now / lax.psum(jnp.sum(direction * image), ("lon", "lat"))
        pressure = pressure + alpha * direction
        residual = residual - alpha * image
        norm_next = squares(residual)
        direction = residual + norm_next / norm_now * direction
        norm_now = norm_next
    adjoint_state = cotangent + inv_root * live_cells * pressure
    features = jnp.concatenate([state, state_lap], axis=0).astype(jnp.bfloat16)
    closure_grad = (CLOSURE_STEP * live_cells * adjoint_state).astype(jnp.bfloat16)
    state_term = adjoint_state + DIFFUSE * laplace(adjoint_state, weights, fold_partner)
    feature_grad, grad_in, grad_out, grad_bias = closure_backward(
        features, closure_grad, weight_in, weight_out, bias_hidden
    )
    adjoint_in = state_term + feature_grad[:L] + laplace(feature_grad[L:], weights, fold_partner)
    grad_in, grad_out, grad_bias = lax.psum((grad_in, grad_out, grad_bias), ("lon", "lat"))
    scale = 1.0 / math.sqrt(row_count * lax.axis_size("lat") * col_count * lax.axis_size("lon"))
    return (adjoint_in, grad_in * scale, grad_out * scale, grad_bias * scale)


def solution(mesh):
    placed = (
        P("ens", "lat", "lon"),
        P("ens", "lat", "lon"),
        P("lat", "lon"),
        P("lat", "lon"),
        P("lon"),
        P(),
        P(),
        P(),
    )
    return jax.shard_map(
        on_device,
        mesh=mesh,
        in_specs=placed,
        out_specs=(P("ens", "lat", "lon"), P("ens", None), P("ens", None), P("ens")),
        check_vma=False,
    )
```

profile of v0, /device:TPU:0, one launch (start us, length us, event | category | flops | bytes accessed | tf_op | source)
XLA Modules:
  0.0 474.6 jit_solution(2489015275346131287)
XLA Ops:
  2.6 3.0 collective-permute-start.6
  6.3 1.3 collective-permute-start.4
  9.7 1.3 collective-permute-start.5
  11.0 5.7 %collective-permute-start.7 = (f32[1,1,128]{2,1,0:T(1,128)}, f32[1,1,128]{2,1,0:T(1,128)}, u32[]{:S(2)}, u32[]{:S(2)}) collective-permute-start(f32[1,1,128]{2,1,0:T(1,128)} %get-tuple-element.284), channel_id=1, source_target_pairs={{0,1},{1,2},{2,3},{4,5},{5,6},{6,7},{8,9},{9,10},{10,11},{12,13},{... | collective-permute-start | bytes 1544 | tf_op jit(solution)/shard_map/ppermute | solution.py:24
  17.5 3.6 collective-permute-start.1
  21.1 8.4 %all-gather.1 = f32[1,1,512]{2,1,0:T(1,128)S(1)} all-gather(f32[1,1,128]{2,1,0:T(1,128)} %get-tuple-element.284), channel_id=3, replica_groups=mesh['ens'=2,'lon'=4,'lat'=4] {'lon'}, dimensions={2}, use_global_device_ids=true | all-gather | bytes 2560 | tf_op jit(solution)/shard_map/all_gather | solution.py:35
  30.1 15.1 %all-gather = f32[17,1,512]{0,2,1:T(8,128)} all-gather(f32[17,1,128]{0,2,1:T(8,128)S(1)} %copy.388), channel_id=2, replica_groups=mesh['ens'=2,'lon'=4,'lat'=4] {'lon'}, dimensions={2}, use_global_device_ids=true | all-gather | bytes 43520 | tf_op jit(solution)/shard_map/all_gather | solution.py:35
  45.3 1.8 fusion.12
  47.7 1.8 gather_fusion.1
  49.5 2.4 gather_fusion
  51.9 2.2 copy.386
  55.1 1.3 broadcast_select_fusion.2
  56.3 3.8 collective-permute-start
  60.2 1.0 fusion.96
  61.8 1.5 copy.368
  63.3 1.1 copy.362
  64.5 2.1 copy.364
  66.6 1.7 fusion.92
  68.4 2.3 multiply_reduce_fusion.4
  70.8 30.0 %all-reduce.1 = (f32[]{:T(128)}, f32[]{:T(128)}) all-reduce(f32[]{:T(128)} %get-tuple-element.277, f32[]{:T(128)} %get-tuple-element.247), channel_id=1, replica_groups=mesh['ens'=2,'lon'=4,'lat'=4] {'lon','lat'}, use_global_device_ids=true, to_apply=%region_2.3 | all-reduce | flops 2 | bytes 16 | tf_op jit(solution)/shard_map/psum | solution.py:54
  101.9 2.1 multiply_reduce_fusion.3
  104.0 30.2 %psum.65 = f32[]{:T(128)} all-reduce(f32[]{:T(128)} %get-tuple-element.245), channel_id=1, replica_groups=mesh['ens'=2,'lon'=4,'lat'=4] {'lon','lat'}, use_global_device_ids=true, to_apply=%region_7.9 | all-reduce | flops 1 | bytes 8 | tf_op jit(solution)/shard_map/psum | solution.py:54
  137.6 1.3 collective-permute-start.10
  138.9 3.5 collective-permute-start.11
  142.5 3.3 fusion.109
  145.8 9.8 %all-gather.2 = f32[1,1,512]{2,1,0:T(1,128)S(1)} all-gather(f32[1,1,128]{2,1,0:T(1,128)} %get-tuple-element.276), channel_id=4, replica_groups=mesh['ens'=2,'lon'=4,'lat'=4] {'lon'}, dimensions={2}, use_global_device_ids=true | all-gather | bytes 2560 | tf_op jit(solution)/shard_map/all_gather | solution.py:35
  155.6 1.4 gather_fusion.2
  157.7 5.6 %collective-permute-done.9 = f32[1,128,1]{2,1,0:T(8,128)S(1)} collective-permute-done((f32[1,128,1]{2,1,0:T(8,128)}, f32[1,128,1]{2,1,0:T(8,128)S(1)}, u32[]{:S(2)}, u32[]{:S(2)}) %collective-permute-start.9) | collective-permute-done | bytes 544 | tf_op jit(solution)/shard_map/ppermute | solution.py:24
  163.3 1.9 multiply_reduce_fusion.2
  165.2 30.1 %psum.66 = f32[]{:T(128)} all-reduce(f32[]{:T(128)} %get-tuple-element.243), channel_id=1, replica_groups=mesh['ens'=2,'lon'=4,'lat'=4] {'lon','lat'}, use_global_device_ids=true, to_apply=%region_9.11 | all-reduce | flops 1 | bytes 8 | tf_op jit(solution)/shard_map/psum | solution.py:124
  197.2 1.1 pad_maximum_fusion.13
  198.3 30.2 %psum.67 = f32[]{:T(128)} all-reduce(f32[]{:T(128)} %multiply_reduce_fusion.1), channel_id=1, replica_groups=mesh['ens'=2,'lon'=4,'lat'=4] {'lon','lat'}, use_global_device_ids=true, to_apply=%region_11.13 | all-reduce | flops 1 | bytes 8 | tf_op jit(solution)/shard_map/psum | solution.py:54
  230.1 1.4 collective-permute-start.14
  231.5 3.0 collective-permute-start.15
  234.6 7.5 %all-gather.3 = f32[1,1,512]{2,1,0:T(1,128)S(1)} all-gather(f32[1,1,128]{2,1,0:T(1,128)S(1)} %get-tuple-element.270), channel_id=5, replica_groups=mesh['ens'=2,'lon'=4,'lat'=4] {'lon'}, dimensions={2}, use_global_device_ids=true | all-gather | bytes 2560 | tf_op jit(solution)/shard_map/all_gather | solution.py:35
  242.1 1.4 gather_fusion.3
  243.5 2.1 collective-permute-start.12
  245.6 2.2 collective-permute-done.12
  247.8 3.8 collective-permute-done.13
  252.4 30.1 %psum.68 = f32[]{:T(128)} all-reduce(f32[]{:T(128)} %fusion.57), channel_id=1, replica_groups=mesh['ens'=2,'lon'=4,'lat'=4] {'lon','lat'}, use_global_device_ids=true, to_apply=%region_13.15 | all-reduce | flops 1 | bytes 8 | tf_op jit(solution)/shard_map/psum | solution.py:124
  284.0 1.1 multiply_convert_fusion
  285.8 69.5 %while.17 = (s32[]{:T(128)}, f32[32,128,128]{2,1,0:T(8,128)S(1)}, f32[32,256]{1,0:T(8,128)S(1)}, f32[256,16]{0,1:T(8,128)S(1)}, f32[256]{0:T(256)S(1)}, /*index=...) while((s32[]{:T(128)}, f32[32,128,128]{2,1,0:T(8,128)S(1)}, ...), condition=%wide.region_16.19_spmd.clone, body=%wide.region_14.18_spmd.clone.sunk | while | flops 68968704 | bytes 5911783 | solution.py:97
  355.4 2.4 collective-permute-start.23
  357.8 7.9 %all-gather.5 = f32[16,1,512]{2,1,0:T(1,128)S(1)} all-gather(f32[16,1,128]{2,1,0:T(1,128)S(1)} %slice.249), channel_id=7, replica_groups=mesh['ens'=2,'lon'=4,'lat'=4] {'lon'}, dimensions={2}, use_global_device_ids=true | all-gather | bytes 40960 | tf_op jit(solution)/shard_map/all_gather | solution.py:35
  365.6 1.1 slice.243
  366.7 1.1 slice.248
  367.8 1.1 slice.289
  368.9 2.0 copy.376
  370.9 2.5 copy.382
  373.5 1.7 fusion.108
  375.2 57.7 %all-reduce = (f32[32,256]{1,0:T(8,128)S(1)}, f32[256,16]{0,1:T(8,128)S(1)}, f32[256]{0:T(256)S(1)}) all-reduce(f32[32,256]{1,0:T(8,128)S(1)} %get-tuple-element.67, f32[256,16]{0,1:T(8,128)S(1)} %get-tuple-element.68, f32[256]{0:T(256)S(1)} %get-tuple-element.69), channel_id=1, replica_groups=mesh['ens'=2,'lon'=4,'lat'=4] {'lon','lat'}, use_global_device_ids=true, to_apply=%region_17.20 | all-reduce | flops 12544 | bytes 100352 | tf_op jit(solution)/shard_map/psum | solution.py:138
  434.7 1.3 collective-permute-start.18
  436.0 3.6 collective-permute-start.19
  442.0 1.3 collective-permute-start.22
  443.3 11.6 %all-gather.4 = f32[16,1,512]{2,1,0:T(1,128)S(1)} all-gather(f32[16,1,128]{2,1,0:T(1,128)S(1)} %get-tuple-element.263), channel_id=6, replica_groups=mesh['ens'=2,'lon'=4,'lat'=4] {'lon'}, dimensions={2}, use_global_device_ids=true | all-gather | bytes 40960 | tf_op jit(solution)/shard_map/all_gather | solution.py:35
  455.9 1.6 copy.369
  457.5 1.6 copy.371
  459.1 2.0 collective-permute-start.17
  461.1 1.9 collective-permute-start.16
  463.0 1.4 copy.379
  464.4 1.4 copy.377
  465.8 1.3 copy.370
  467.1 1.3 copy.372
  468.5 6.1 %fusion.18 = f32[16,128,128]{2,1,0:T(8,128)} fusion(f32[16,128,128]{2,1,0:T(8,128)} %slice.243, f32[16,1,128]{2,1,0:T(1,128)} %collective-permute-done.23, f32[16,128,1]{2,1,0:T(8,128)} %copy.379, f32[16,128,1]{2,1,0:T(8,128)} %copy.377, f32[16,128,128]{2,1,0:T(8,128)S(1)} %get-tuple-element.242, f32[16,1,128]{2,1,0:T(1,128)} %collective-permute-done.19, ...), kind=kLoop, calls=%fused_computation.38 | loop fusion | flops 8912896 | bytes 6602752 | tf_op jit(solution)/shard_map/add | solution.py:137
  (338 shorter events, 77.3 us)
Async XLA Ops:
  0.6 7.0 %copy-start.32 = (s32[128,128]{1,0:T(8,128)S(1)}, s32[128,128]{1,0:T(8,128)}, u32[]{:S(2)}) copy-start(s32[128,128]{1,0:T(8,128)} %param.17) | copy-start | bytes 196612
  0.6 7.0 %copy-start.2 = (f32[16,128,128]{2,1,0:T(8,128)S(1)}, f32[16,128,128]{2,1,0:T(8,128)}, u32[]{:S(2)}) copy-start(f32[16,128,128]{2,1,0:T(8,128)} %param.15) | copy-start | bytes 3145732
  1.6 6.9 %copy-start.26 = (f32[128,128]{1,0:T(8,128)}, f32[128,128]{1,0:T(8,128)S(1)}, u32[]{:S(2)}) copy-start(f32[128,128]{1,0:T(8,128)S(1)} %get-tuple-element.286) | copy-start | bytes 196612
  2.6 59.2 %collective-permute-start.6 = (f32[17,1,128]{0,2,1:T(8,128)S(1)}, f32[17,1,128]{0,2,1:T(8,128)}, u32[]{:S(2)}, u32[]{:S(2)}) collective-permute-start(f32[17,1,128]{0,2,1:T(8,128)S(1)} %copy.388), channel_id=1, source_target_pairs={{0,1},{1,2},{2,3},{4,5},{5,6},{6,7},{8,9},{9,10},{10,11},{12,13},{... | collective-permute-start | bytes 26120 | tf_op jit(solution)/shard_map/ppermute | solution.py:24
  5.6 39.6 %copy-start = (f32[16,128,128]{2,1,0:T(8,128)S(1)}, f32[16,128,128]{2,1,0:T(8,128)}, u32[]{:S(2)}) copy-start(f32[16,128,128]{2,1,0:T(8,128)} %param.14) | copy-start | bytes 3145732
  6.3 50.0 %collective-permute-start.4 = (f32[17,1,128]{0,2,1:T(8,128)}, f32[17,1,128]{0,2,1:T(8,128)}, u32[]{:S(2)}, u32[]{:S(2)}) collective-permute-start(f32[17,1,128]{0,2,1:T(8,128)} %copy.389), channel_id=1, source_target_pairs={{1,0},{2,1},{3,2},{5,4},{6,5},{7,6},{9,8},{10,9},{11,10},{13,12},{... | collective-permute-start | bytes 26120 | tf_op jit(solution)/shard_map/ppermute | solution.py:27
  9.7 45.3 %collective-permute-start.5 = (f32[1,1,128]{2,1,0:T(1,128)}, f32[1,1,128]{2,1,0:T(1,128)}, u32[]{:S(2)}, u32[]{:S(2)}) collective-permute-start(f32[1,1,128]{2,1,0:T(1,128)} %get-tuple-element.283), channel_id=1, source_target_pairs={{1,0},{2,1},{3,2},{5,4},{6,5},{7,6},{9,8},{10,9},{11,10},{13,12},{... | collective-permute-start | bytes 1544 | tf_op jit(solution)/shard_map/ppermute | solution.py:27
  11.0 57.3 %collective-permute-start.7 = (f32[1,1,128]{2,1,0:T(1,128)}, f32[1,1,128]{2,1,0:T(1,128)}, u32[]{:S(2)}, u32[]{:S(2)}) collective-permute-start(f32[1,1,128]{2,1,0:T(1,128)} %get-tuple-element.284), channel_id=1, source_target_pairs={{0,1},{1,2},{2,3},{4,5},{5,6},{6,7},{8,9},{9,10},{10,11},{12,13},{... | collective-permute-start | bytes 1544 | tf_op jit(solution)/shard_map/ppermute | solution.py:24
  17.5 50.9 %collective-permute-start.1 = (f32[1,128,1]{2,1,0:T(8,128)}, f32[1,128,1]{2,1,0:T(8,128)}, u32[]{:S(2)}, u32[]{:S(2)}) collective-permute-start(f32[1,128,1]{2,1,0:T(8,128)} %get-tuple-element.281), channel_id=1, source_target_pairs={{4,0},{8,4},{12,8},{0,12},{5,1},{9,5},{13,9},{1,13},{6,2},{10,6},{... | collective-permute-start | bytes 1544 | tf_op jit(solution)/shard_map/ppermute | solution.py:27
  45.3 1.8 copy-start.43
  49.5 4.6 copy-start.1
  55.1 9.4 %collective-permute-start.2 = (f32[17,128,1]{1,2,0:T(1,128)}, f32[17,128,1]{1,2,0:T(1,128)}, u32[]{:S(2)}, u32[]{:S(2)}) collective-permute-start(f32[17,128,1]{1,2,0:T(1,128)} %copy.387), channel_id=1, source_target_pairs={{0,4},{4,8},{8,12},{12,0},{1,5},{5,9},{9,13},{13,1},{2,6},{6,10},{... | collective-permute-start | bytes 26120 | tf_op jit(solution)/shard_map/ppermute | solution.py:24
  56.3 7.0 %copy-start.38 = (pred[128]{0:T(512)(128)(4,1)}, pred[128]{0:T(512)(128)(4,1)S(1)}, u32[]{:S(2)}) copy-start(pred[128]{0:T(512)(128)(4,1)S(1)} %get-tuple-element.250) | copy-start | bytes 388
  56.3 7.0 %collective-permute-start = (f32[17,128,1]{1,2,0:T(1,128)}, f32[17,128,1]{1,2,0:T(1,128)}, u32[]{:S(2)}, u32[]{:S(2)}) collective-permute-start(f32[17,128,1]{1,2,0:T(1,128)} %copy.386), channel_id=1, source_target_pairs={{4,0},{8,4},{12,8},{0,12},{5,1},{9,5},{13,9},{1,13},{6,2},{10,6},{... | collective-permute-start | bytes 26120 | tf_op jit(solution)/shard_map/ppermute | solution.py:27
  61.8 6.6 %collective-permute-start.3 = (f32[1,128,1]{2,1,0:T(8,128)}, f32[1,128,1]{2,1,0:T(8,128)}, u32[]{:S(2)}, u32[]{:S(2)}) collective-permute-start(f32[1,128,1]{2,1,0:T(8,128)} %get-tuple-element.282), channel_id=1, source_target_pairs={{0,4},{4,8},{8,12},{12,0},{1,5},{5,9},{9,13},{13,1},{2,6},{6,10},{... | collective-permute-start | bytes 1544 | tf_op jit(solution)/shard_map/ppermute | solution.py:24
  63.3 3.2 copy-start.6
  66.6 1.8 copy-start.20
  66.6 1.8 copy-start.28
  66.6 1.8 copy-start.30
  66.6 1.8 copy-start.34
  66.6 1.8 copy-start.42
  68.3 2.4 copy-start.10
  68.3 2.4 copy-start.12
  68.3 2.4 copy-start.14
  68.3 2.4 copy-start.16
  68.3 2.4 copy-start.18
  137.6 19.4 %collective-permute-start.10 = (f32[1,1,128]{2,1,0:T(1,128)}, f32[1,1,128]{2,1,0:T(1,128)}, u32[]{:S(2)}, u32[]{:S(2)}) collective-permute-start(f32[1,1,128]{2,1,0:T(1,128)} %get-tuple-element.275), channel_id=1, source_target_pairs={{1,0},{2,1},{3,2},{5,4},{6,5},{7,6},{9,8},{10,9},{11,10},{13,12},{... | collective-permute-start | bytes 1544 | tf_op jit(solution)/shard_map/ppermute | solution.py:27
  138.9 18.8 %collective-permute-start.11 = (f32[1,1,128]{2,1,0:T(1,128)}, f32[1,1,128]{2,1,0:T(1,128)}, u32[]{:S(2)}, u32[]{:S(2)}) collective-permute-start(f32[1,1,128]{2,1,0:T(1,128)} %get-tuple-element.276), channel_id=1, source_target_pairs={{0,1},{1,2},{2,3},{4,5},{5,6},{6,7},{8,9},{9,10},{10,11},{12,13},{... | collective-permute-start | bytes 1544 | tf_op jit(solution)/shard_map/ppermute | solution.py:24
  142.4 15.3 %collective-permute-start.8 = (f32[1,128,1]{2,1,0:T(8,128)}, f32[1,128,1]{2,1,0:T(8,128)}, u32[]{:S(2)}, u32[]{:S(2)}) collective-permute-start(f32[1,128,1]{2,1,0:T(8,128)} %get-tuple-element.273), channel_id=1, source_target_pairs={{4,0},{8,4},{12,8},{0,12},{5,1},{9,5},{13,9},{1,13},{6,2},{10,6},{... | collective-permute-start | bytes 1544 | tf_op jit(solution)/shard_map/ppermute | solution.py:27
  145.8 50.7 %copy-start.8 = (f32[1,128,128]{2,1,0:T(8,128)S(1)}, f32[1,128,128]{2,1,0:T(8,128)}, u32[]{:S(2)}) copy-start(f32[1,128,128]{2,1,0:T(8,128)} %get-tuple-element.246) | copy-start | bytes 196612
  145.8 51.4 %copy-start.4 = (bf16[16,128,128]{2,1,0:T(8,128)(2,1)S(1)}, bf16[16,128,128]{2,1,0:T(8,128)(2,1)}, u32[]{:S(2)}) copy-start(bf16[16,128,128]{2,1,0:T(8,128)(2,1)} %get-tuple-element.266) | copy-start | bytes 1572868
  145.8 51.4 %copy-start.5 = (bf16[16,128,128]{2,1,0:T(8,128)(2,1)S(1)}, bf16[16,128,128]{2,1,0:T(8,128)(2,1)}, u32[]{:S(2)}) copy-start(bf16[16,128,128]{2,1,0:T(8,128)(2,1)} %get-tuple-element.267) | copy-start | bytes 1572868
  157.0 6.3 %collective-permute-start.9 = (f32[1,128,1]{2,1,0:T(8,128)}, f32[1,128,1]{2,1,0:T(8,128)S(1)}, u32[]{:S(2)}, u32[]{:S(2)}) collective-permute-start(f32[1,128,1]{2,1,0:T(8,128)} %get-tuple-element.274), channel_id=1, source_target_pairs={{0,4},{4,8},{8,12},{12,0},{1,5},{5,9},{9,13},{13,1},{2,6},{6,10},{... | collective-permute-start | bytes 1544 | tf_op jit(solution)/shard_map/ppermute | solution.py:24
  198.3 47.4 %copy-start.39 = (pred[128]{0:T(512)(128)(4,1)S(1)}, pred[128]{0:T(512)(128)(4,1)}, u32[]{:S(2)}) copy-start(pred[128]{0:T(512)(128)(4,1)} %copy-done.38) | copy-start | bytes 388
  198.3 53.4 %copy-start.11 = (f32[1,128,128]{2,1,0:T(8,128)S(1)}, f32[1,128,128]{2,1,0:T(8,128)}, u32[]{:S(2)}) copy-start(f32[1,128,128]{2,1,0:T(8,128)} %copy-done.10) | copy-start | bytes 196612
  198.3 53.4 %copy-start.13 = (f32[1,128,128]{2,1,0:T(8,128)S(1)}, f32[1,128,128]{2,1,0:T(8,128)}, u32[]{:S(2)}) copy-start(f32[1,128,128]{2,1,0:T(8,128)} %copy-done.12) | copy-start | bytes 196612
  198.3 53.4 %copy-start.15 = (f32[1,128,128]{2,1,0:T(8,128)S(1)}, f32[1,128,128]{2,1,0:T(8,128)}, u32[]{:S(2)}) copy-start(f32[1,128,128]{2,1,0:T(8,128)} %copy-done.14) | copy-start | bytes 196612
  198.3 53.4 %copy-start.17 = (f32[1,128,128]{2,1,0:T(8,128)S(1)}, f32[1,128,128]{2,1,0:T(8,128)}, u32[]{:S(2)}) copy-start(f32[1,128,128]{2,1,0:T(8,128)} %copy-done.16) | copy-start | bytes 196612
  198.3 53.4 %copy-start.19 = (f32[1,128,128]{2,1,0:T(8,128)S(1)}, f32[1,128,128]{2,1,0:T(8,128)}, u32[]{:S(2)}) copy-start(f32[1,128,128]{2,1,0:T(8,128)} %copy-done.18) | copy-start | bytes 196612
  198.3 53.4 %copy-start.21 = (f32[128,128]{1,0:T(8,128)S(1)}, f32[128,128]{1,0:T(8,128)}, u32[]{:S(2)}) copy-start(f32[128,128]{1,0:T(8,128)} %get-tuple-element.204) | copy-start | bytes 196612
  198.3 53.4 %copy-start.29 = (f32[17,1,128]{2,1,0:T(1,128)S(1)}, f32[17,1,128]{2,1,0:T(1,128)}, u32[]{:S(2)}) copy-start(f32[17,1,128]{2,1,0:T(1,128)} %copy.367) | copy-start | bytes 26116
  198.3 53.4 %copy-start.31 = (f32[17,1,128]{2,1,0:T(1,128)S(1)}, f32[17,1,128]{2,1,0:T(1,128)}, u32[]{:S(2)}) copy-start(f32[17,1,128]{2,1,0:T(1,128)} %copy.368) | copy-start | bytes 26116
  229.9 54.0 %copy-start.3 = (f32[16,128,128]{2,1,0:T(8,128)S(1)}, f32[16,128,128]{2,1,0:T(8,128)}, u32[]{:S(2)}) copy-start(f32[16,128,128]{2,1,0:T(8,128)} %param.15) | copy-start | bytes 3145732
  230.0 54.0 %copy-start.27 = (f32[128,128]{1,0:T(8,128)S(1)}, f32[128,128]{1,0:T(8,128)}, u32[]{:S(2)}) copy-start(f32[128,128]{1,0:T(8,128)} %copy-done.26) | copy-start | bytes 196612
  230.0 54.0 %copy-start.33 = (s32[128,128]{1,0:T(8,128)S(1)}, s32[128,128]{1,0:T(8,128)}, u32[]{:S(2)}) copy-start(s32[128,128]{1,0:T(8,128)} %param.17) | copy-start | bytes 196612
  230.1 15.5 %collective-permute-start.14 = (f32[1,1,128]{2,1,0:T(1,128)S(1)}, f32[1,1,128]{2,1,0:T(1,128)S(1)}, u32[]{:S(2)}, u32[]{:S(2)}) collective-permute-start(f32[1,1,128]{2,1,0:T(1,128)S(1)} %get-tuple-element.269), channel_id=1, source_target_pairs={{1,0},{2,1},{3,2},{5,4},{6,5},{7,6},{9,8},{10,9},{11,10},{13,12},{... | collective-permute-start | bytes 1544 | tf_op jit(solution)/shard_map/ppermute | solution.py:27
  231.5 14.1 %collective-permute-start.15 = (f32[1,1,128]{2,1,0:T(1,128)S(1)}, f32[1,1,128]{2,1,0:T(1,128)S(1)}, u32[]{:S(2)}, u32[]{:S(2)}) collective-permute-start(f32[1,1,128]{2,1,0:T(1,128)S(1)} %get-tuple-element.270), channel_id=1, source_target_pairs={{0,1},{1,2},{2,3},{4,5},{5,6},{6,7},{8,9},{9,10},{10,11},{12,13},{... | collective-permute-start | bytes 1544 | tf_op jit(solution)/shard_map/ppermute | solution.py:24
  243.5 4.3 collective-permute-start.12
  245.5 6.1 %collective-permute-start.13 = (f32[1,128,1]{2,1,0:T(8,128)S(1)}, f32[1,128,1]{2,1,0:T(8,128)S(1)}, u32[]{:S(2)}, u32[]{:S(2)}) collective-permute-start(f32[1,128,1]{2,1,0:T(8,128)S(1)} %get-tuple-element.272), channel_id=1, source_target_pairs={{0,4},{4,8},{8,12},{12,0},{1,5},{5,9},{9,13},{13,1},{2,6},{6,10},{... | collective-permute-start | bytes 1544 | tf_op jit(solution)/shard_map/ppermute | solution.py:24
  285.1 0.8 copy-start.35
  285.1 0.8 copy-start.36
  355.4 113.1 %collective-permute-start.23 = (f32[16,1,128]{2,1,0:T(1,128)S(1)}, f32[16,1,128]{2,1,0:T(1,128)}, u32[]{:S(2)}, u32[]{:S(2)}) collective-permute-start(f32[16,1,128]{2,1,0:T(1,128)S(1)} %slice.249), channel_id=1, source_target_pairs={{0,1},{1,2},{2,3},{4,5},{5,6},{6,7},{8,9},{9,10},{10,11},{12,13},{... | collective-permute-start | bytes 24584 | tf_op jit(solution)/shard_map/ppermute | solution.py:24
  434.7 24.3 %collective-permute-start.18 = (f32[16,1,128]{2,0,1:T(8,128)S(1)}, f32[16,1,128]{2,0,1:T(8,128)S(1)}, u32[]{:S(2)}, u32[]{:S(2)}) collective-permute-start(f32[16,1,128]{2,0,1:T(8,128)S(1)} %bitcast.253), channel_id=1, source_target_pairs={{1,0},{2,1},{3,2},{5,4},{6,5},{7,6},{9,8},{10,9},{11,10},{13,12},{... | collective-permute-start | bytes 24584 | tf_op jit(solution)/shard_map/ppermute | solution.py:27
  436.0 32.5 %collective-permute-start.19 = (f32[16,1,128]{2,1,0:T(1,128)S(1)}, f32[16,1,128]{2,1,0:T(1,128)}, u32[]{:S(2)}, u32[]{:S(2)}) collective-permute-start(f32[16,1,128]{2,1,0:T(1,128)S(1)} %get-tuple-element.263), channel_id=1, source_target_pairs={{0,1},{1,2},{2,3},{4,5},{5,6},{6,7},{8,9},{9,10},{10,11},{12,13},{... | collective-permute-start | bytes 24584 | tf_op jit(solution)/shard_map/ppermute | solution.py:24
  441.3 17.8 %collective-permute-start.21 = (f32[16,128,1]{1,0,2:T(8,128)S(1)}, f32[16,128,1]{1,0,2:T(8,128)S(1)}, u32[]{:S(2)}, u32[]{:S(2)}) collective-permute-start(f32[16,128,1]{1,0,2:T(8,128)S(1)} %get-tuple-element.254), channel_id=1, source_target_pairs={{0,4},{4,8},{8,12},{12,0},{1,5},{5,9},{9,13},{13,1},{2,6},{6,10},{... | collective-permute-start | bytes 24584 | tf_op jit(solution)/shard_map/ppermute | solution.py:24
  442.0 19.1 %collective-permute-start.22 = (f32[16,1,128]{2,0,1:T(8,128)S(1)}, f32[16,1,128]{2,0,1:T(8,128)S(1)}, u32[]{:S(2)}, u32[]{:S(2)}) collective-permute-start(f32[16,1,128]{2,0,1:T(8,128)S(1)} %slice.294), channel_id=1, source_target_pairs={{1,0},{2,1},{3,2},{5,4},{6,5},{7,6},{9,8},{10,9},{11,10},{13,12},{... | collective-permute-start | bytes 24584 | tf_op jit(solution)/shard_map/ppermute | solution.py:27
  455.8 7.1 %copy-start.40 = (pred[128]{0:T(512)(128)(4,1)S(1)}, pred[128]{0:T(512)(128)(4,1)}, u32[]{:S(2)}) copy-start(pred[128]{0:T(512)(128)(4,1)} %copy-done.38) | copy-start | bytes 388
  459.0 5.3 %collective-permute-start.20 = (f32[16,128,1]{1,0,2:T(8,128)S(1)}, f32[16,128,1]{1,0,2:T(8,128)S(1)}, u32[]{:S(2)}, u32[]{:S(2)}) collective-permute-start(f32[16,128,1]{1,0,2:T(8,128)S(1)} %get-tuple-element.253), channel_id=1, source_target_pairs={{4,0},{8,4},{12,8},{0,12},{5,1},{9,5},{13,9},{1,13},{6,2},{10,6},{... | collective-permute-start | bytes 24584 | tf_op jit(solution)/shard_map/ppermute | solution.py:27
  459.1 8.0 %collective-permute-start.17 = (f32[16,128,1]{1,0,2:T(8,128)S(1)}, f32[16,128,1]{1,0,2:T(8,128)S(1)}, u32[]{:S(2)}, u32[]{:S(2)}) collective-permute-start(f32[16,128,1]{1,0,2:T(8,128)S(1)} %copy.371), channel_id=1, source_target_pairs={{0,4},{4,8},{8,12},{12,0},{1,5},{5,9},{9,13},{13,1},{2,6},{6,10},{... | collective-permute-start | bytes 24584 | tf_op jit(solution)/shard_map/ppermute | solution.py:24
  461.1 4.6 collective-permute-start.16
  465.7 2.7 copy-start.22
  465.7 2.7 copy-start.23
  465.7 2.7 copy-start.24
  465.7 2.7 copy-start.25
  (4 other events, 2.9 us)
where the time goes:
time: 478 us; the launch traced here: 475 us
  blocking collectives  269 us (56%)
  local copies, waits for them, and re-layouts  78.8 us (16%)
  starting transfers between devices  42.6 us (9%)
  other arithmetic  32.1 us (7%)
  matrix products  21.8 us (5%)
  waiting for transfers between devices  11.6 us (2%)
  loops' own time  11.4 us (2%)
  between operations  7.79 us (2%)
    psum x3, blocking collectives, squares(): return lax.psum(jnp.sum(residual * residual), ('lon', 'lat'))  90.4 us
    all_gather x6, blocking collectives, neighbours(): top_row = lax.all_gather(grid_field[:, -1, :], 'lon', axis=1, tiled=True)  60.3 us
    psum x2, blocking collectives, on_device(): alpha = norm_now / lax.psum(jnp.sum(direction * image), ('lon', 'lat'))  60.2 us
    psum x1, blocking collectives, on_device(): lax.psum((grad_in, grad_out, grad_bias), ('lon', 'lat'))  57.7 us
    ppermute x12, starting transfers between devices, with_halo(): lax.ppermute(lax.slice_in_dim(block, block.shape[dim] - width, None, axis...  23.4 us
    ppermute x12, starting transfers between devices, with_halo(): lax.ppermute(lax.slice_in_dim(block, 0, width, axis=dim), axis, backward)  19.2 us
    dynamic_slice x16, local copies, waits for them, and re-layouts, one_block(): lax.dynamic_slice_in_dim(features, start, 8, 1)  13.5 us
    dynamic_slice x16, local copies, waits for them, and re-layouts, one_block(): lax.dynamic_slice_in_dim(closure_grad, start, 8, 1)  12.3 us
  transfers between devices with their start and end apart: 24, of which 3 were waited for; matrix products, arithmetic and copies ran while one was open for 11% of the time, Pallas kernels for 0%

commit v1 on v0

v1 whole, which is shorter than its diff:
```python
import functools
import math

import jax
import jax.numpy as jnp
from jax import lax
from jax.experimental import pallas as pl
from jax.experimental.pallas import tpu as pltpu
from jax.sharding import PartitionSpec as P

L = 16
H = 256
DIFFUSE = 0.2
CLOSURE_STEP = 0.5
F32 = jnp.float32
BF16 = jnp.bfloat16
MESH = pl.DeviceIdType.MESH

SHIFT = 4.25
SPAN = 4.15
TILES = 16
GROUP = 4


def fold_select(fold, lon, block, width, east_lanes, size):
    source = lax.broadcasted_iota(jnp.int32, (128, width), 0) + block * 128
    lane = lax.broadcasted_iota(jnp.int32, (128, width), 1)
    column = jnp.where(lane < east_lanes, lane, lane - 256) + lon * 128
    centre = fold[0:1, 0:1] + lon * 128
    total = source + column - centre
    hit = total == 0
    for turns in (-2, -1, 1, 2):
        hit = hit | (total == turns * size)
    return jnp.where(hit, 1.0, 0.0).astype(F32)


def exact_dot(a, b, dims=(((1,), (0,)), ((), ()))):
    return lax.dot_general(
        a, b, dims, precision=lax.Precision.HIGHEST, preferred_element_type=F32
    )


def dot_nt(a, b):
    return lax.dot_general(a, b, (((1,), (1,)), ((), ())), preferred_element_type=F32)


def krylov_coefficients(moments):
    zero = jnp.zeros_like(moments[0])

    def inner(a, b):
        total = zero
        for i, x in enumerate(a):
            for j, y in enumerate(b):
                if x is not None and y is not None:
                    total = total + x * y * moments[i + j]
        return total

    one = zero + 1.0
    residual = [one]
    direction = [one]
    pressure = [zero, zero, zero]
    norm_now = moments[0]
    for step in range(3):
        image = [SHIFT * d for d in direction] + [zero]
        image = [
            x + (SPAN * direction[k - 1] if k > 0 else zero) for k, x in enumerate(image)
        ]
        alpha = norm_now / inner(direction, image)
        alpha = jnp.minimum(jnp.maximum(alpha, 1.0 / 8.41), 10.01)
        pressure = [
            x + (alpha * direction[k] if k < len(direction) else zero)
            for k, x in enumerate(pressure)
        ]
        if step == 2:
            break
        residual = residual + [zero]
        residual = [x - alpha * y for x, y in zip(residual, image)]
        norm_next = jnp.maximum(inner(residual, residual), 0.0)
        beta = norm_next / norm_now
        direction = direction + [zero]
        direction = [x + beta * y for x, y in zip(residual, direction)]
        norm_now = norm_next
    return pressure


def kernel(
    nlat, nlon,
    state, cot, mask, count, fold, w_in, w_out, bias,
    out, g_in, g_out, g_bias,
    xt, zt, yt, feat, bext, cext, wts, basis, pres, w_in_t, bias_b, bias_acc,
    gi_acc, go_acc,
    msg, recv, diag, top, zmsg, zrecv, ztop,
    mom, mom_lat, mom_lon, gpart, g_rs, g_own, g_lon, g_full,
    e_send, e_recv, d_send, d_recv, t_send, t_recv,
    ml_send, ml_recv, mo_send, mo_recv,
    z_send, z_recv, zt_send, zt_recv,
    rs_send, rs_recv, gl_send, gl_recv, ag_send, ag_recv,
):
    rows = mask.shape[0]
    size_lon = nlon * 128
    lat = lax.axis_index("lat")
    lon = lax.axis_index("lon")
    at_top = lat == nlat - 1
    has_south = lat > 0
    has_north = lat < nlat - 1
    south = lax.rem(lat + nlat - 1, nlat)
    north = lax.rem(lat + 1, nlat)
    west = lax.rem(lon + nlon - 1, nlon)
    east = lax.rem(lon + 1, nlon)

    def lat_peer(d):
        return lax.rem(lat + d, nlat)

    def lon_peer(d):
        return lax.rem(lon + d, nlon)

    barrier = pltpu.get_barrier_semaphore()
    for d in range(1, nlat):
        pl.semaphore_signal(barrier, inc=1, device_id={"lat": lat_peer(d)}, device_id_type=MESH)
    for d in range(1, nlon):
        pl.semaphore_signal(barrier, inc=1, device_id={"lon": lon_peer(d)}, device_id_type=MESH)

    @pl.when(has_south)
    def _():
        for side in (west, east):
            pl.semaphore_signal(
                barrier, inc=1, device_id={"lat": south, "lon": side}, device_id_type=MESH
            )

    @pl.when(has_north)
    def _():
        for side in (west, east):
            pl.semaphore_signal(
                barrier, inc=1, device_id={"lat": north, "lon": side}, device_id_type=MESH
            )

    mask_f = mask[...].astype(F32)
    live_count = mask_f * count[...].astype(F32)
    total = jnp.zeros((rows, 128), F32)
    for k in range(L):
        total = total + jnp.where(live_count > k, cot[k * rows:(k + 1) * rows, :], 0.0)
    right = (-1.0 / math.sqrt(L)) * total
    bext[8:8 + rows, 0:128] = right
    cext[8:8 + rows, 0:128] = live_count
    right_t = right.T
    count_t = live_count.T

    lane = lax.broadcasted_iota(jnp.int32, (L, 128), 1)
    level = lax.broadcasted_iota(jnp.int32, (L, 128), 0).astype(F32)

    def transpose_rows(i, carry):
        low, high = carry
        for k in range(8):
            r = i * 8 + k
            x = state[pl.ds(r, L, stride=rows), :]
            xt[r + 1] = x
            low = jnp.where(lane == r, x[:, 0:1], low)
            high = jnp.where(lane == r, x[:, 127:128], high)
        return low, high

    zeros = jnp.zeros((L, 128), F32)
    low, high = lax.fori_loop(0, rows // 8, transpose_rows, (zeros, zeros))

    msg[0, 0:16] = xt[1]
    msg[0, 16:24] = right[0:8]
    msg[0, 24:32] = live_count[0:8]
    msg[1, 0:16] = xt[rows]
    msg[1, 16:24] = right[rows - 8:rows]
    msg[1, 24:32] = live_count[rows - 8:rows]
    msg[2, 0:16] = low
    msg[2, 16:24] = right_t[0:8]
    msg[2, 24:32] = count_t[0:8]
    msg[3, 0:16] = high
    msg[3, 16:24] = right_t[120:128]
    msg[3, 24:32] = count_t[120:128]

    waits = (nlat - 1) + (nlon - 1) + 2 * has_south.astype(jnp.int32) + 2 * has_north.astype(jnp.int32)
    pl.semaphore_wait(barrier, waits)

    def remote(src, dst, send, receive, device):
        return pltpu.make_async_remote_copy(
            src_ref=src, dst_ref=dst, send_sem=send, recv_sem=receive,
            device_id=device, device_id_type=MESH,
        )

    def edge_copies(source, target, send, receive):
        return (
            remote(source.at[0], target.at[1], send.at[0], receive.at[1], {"lat": south}),
            remote(source.at[1], target.at[0], send.at[1], receive.at[0], {"lat": north}),
            remote(source.at[2], target.at[3], send.at[2], receive.at[3], {"lon": west}),
            remote(source.at[3], target.at[2], send.at[3], receive.at[2], {"lon": east}),
        )

    def top_copies(source, target, send, receive):
        return [
            remote(source, target.at[d], send.at[d], receive.at[d], {"lon": lon_peer(d)})
            for d in range(1, nlon)
        ]

    def start_edges(edges, tops):
        edges[2].start()
        edges[3].start()

        @pl.when(has_south)
        def _():
            edges[0].start()

        @pl.when(has_north)
        def _():
            edges[1].start()

        @pl.when(at_top)
        def _():
            for copy in tops:
                copy.start()

    def finish_edges(edges, tops):
        edges[2].wait()
        edges[3].wait()

        @pl.when(has_south)
        def _():
            edges[0].wait_send()
            edges[1].wait_recv()

        @pl.when(has_north)
        def _():
            edges[1].wait_send()
            edges[0].wait_recv()

        @pl.when(at_top)
        def _():
            for copy in tops:
                copy.wait()

    edges = edge_copies(msg, recv, e_send, e_recv)
    tops = top_copies(msg.at[1], top, t_send, t_recv)
    corners = (
        remote(msg.at[0, 16:32], diag.at[3], d_send.at[0], d_recv.at[3], {"lat": south, "lon": west}),
        remote(msg.at[0, 16:32], diag.at[2], d_send.at[1], d_recv.at[2], {"lat": south, "lon": east}),
        remote(msg.at[1, 16:32], diag.at[1], d_send.at[2], d_recv.at[1], {"lat": north, "lon": west}),
        remote(msg.at[1, 16:32], diag.at[0], d_send.at[3], d_recv.at[0], {"lat": north, "lon": east}),
    )
    start_edges(edges, tops)

    @pl.when(has_south)
    def _():
        corners[0].start()
        corners[1].start()

    @pl.when(has_north)
    def _():
        corners[2].start()
        corners[3].start()

    pad = jnp.zeros((96, H), F32)
    w_in_t[...] = jnp.concatenate([w_in[...].astype(F32), pad], axis=0).T[:, 0:32].astype(BF16)
    bias_b[...] = jnp.broadcast_to(bias[...], (128, H)).T
    bias_acc[...] = jnp.zeros_like(bias_acc)
    gi_acc[...] = jnp.zeros_like(gi_acc)
    go_acc[...] = jnp.zeros_like(go_acc)

    finish_edges(edges, tops)

    @pl.when(has_south)
    def _():
        corners[0].wait_send()
        corners[1].wait_send()
        corners[2].wait_recv()
        corners[3].wait_recv()

    @pl.when(has_north)
    def _():
        corners[2].wait_send()
        corners[3].wait_send()
        corners[0].wait_recv()
        corners[1].wait_recv()

    middle = jnp.zeros((112, 128), F32)
    bext[8:8 + rows, 128:256] = jnp.concatenate([recv[3, 16:24], middle, recv[2, 16:24]], axis=0).T
    cext[8:8 + rows, 128:256] = jnp.concatenate([recv[3, 24:32], middle, recv[2, 24:32]], axis=0).T
    near = lax.broadcasted_iota(jnp.int32, (8, 128), 1) < 64

    @pl.when(has_south)
    def _():
        bext[0:8, 0:128] = recv[0, 16:24]
        cext[0:8, 0:128] = recv[0, 24:32]
        bext[0:8, 128:256] = jnp.where(near, diag[1, 0:8], diag[0, 0:8])
        cext[0:8, 128:256] = jnp.where(near, diag[1, 8:16], diag[0, 8:16])
        xt[0] = recv[0, 0:16]

    @pl.when(jnp.logical_not(has_south))
    def _():
        bext[0:8, :] = jnp.zeros((8, 256), F32)
        cext[0:8, :] = jnp.zeros((8, 256), F32)
        xt[0] = zeros

    last = 8 + rows

    @pl.when(has_north)
    def _():
        bext[last:last + 8, 0:128] = recv[1, 16:24]
        cext[last:last + 8, 0:128] = recv[1, 24:32]
        bext[last:last + 8, 128:256] = jnp.where(near, diag[3, 0:8], diag[2, 0:8])
        cext[last:last + 8, 128:256] = jnp.where(near, diag[3, 8:16], diag[2, 8:16])
        xt[rows + 1] = recv[1, 0:16]

    @pl.when(at_top)
    def _():
        folded = exact_dot(msg[1], fold_select(fold[...], lon, lon, 256, 192, size_lon))
        for d in range(1, nlon):
            block = lax.rem(lon + nlon - d, nlon)
            folded = folded + exact_dot(top[d], fold_select(fold[...], lon, block, 256, 192, size_lon))
        xt[rows + 1] = folded[0:16, 0:128]
        for k in range(3):
            bext[last + k:last + k + 1, :] = folded[23 - k:24 - k, :]
            cext[last + k:last + k + 1, :] = folded[31 - k:32 - k, :]
        bext[last + 3:last + 8, :] = jnp.zeros((5, 256), F32)
        cext[last + 3:last + 8, :] = jnp.zeros((5, 256), F32)

    ext = rows + 16
    counts = cext[...]
    ocean = jnp.where(counts > 0.5, 1.0, 0.0).astype(F32)

    def sides(v):
        return (
            pltpu.roll(v, 255, 1), pltpu.roll(v, 1, 1),
            pltpu.roll(v, ext - 1, 0), pltpu.roll(v, 1, 0),
        )

    weights = [ocean * side for side in sides(ocean)]
    weight_sum = weights[0] + weights[1] + weights[2] + weights[3]
    for k in range(4):
        wts[k] = weights[k][8:8 + rows, 0:128]
    wts[4] = weight_sum[8:8 + rows, 0:128]
    wts[5] = live_count
    inv = 1.0 / SPAN
    centre_weight = ((0.1 - SHIFT) + (0.3 / L) * counts + weight_sum) * inv
    weights = [w * inv for w in weights]

    def shifted(v):
        side = sides(v)
        r = centre_weight * v
        for k in range(4):
            r = r - weights[k] * side[k]
        return r

    def own(v):
        return v[8:8 + rows, 0:128]

    def colsum(a, b):
        return jnp.sum(a * b, axis=0, keepdims=True)

    u0 = bext[...]
    u1 = shifted(u0)
    u2 = shifted(u1)
    u3 = own(shifted(u2))
    u0, u1, u2 = own(u0), own(u1), own(u2)
    basis[0] = u0
    basis[1] = u1
    basis[2] = u2
    mom[...] = jnp.concatenate(
        [colsum(u0, u0), colsum(u0, u1), colsum(u1, u1), colsum(u1, u2),
         colsum(u2, u2), colsum(u2, u3), jnp.zeros((2, 128), F32)], axis=0
    )

    mom_lat_copies = [
        remote(mom, mom_lat.at[d], ml_send.at[d], ml_recv.at[d], {"lat": lat_peer(d)})
        for d in range(1, nlat)
    ]
    for copy in mom_lat_copies:
        copy.start()

    def lap_row(field, ghost_west, ghost_east, r):
        x = field[r + 1]
        e = jnp.where(lane == 127, pltpu.roll(ghost_east, 127 - r, 1), pltpu.roll(x, 127, 1))
        w = jnp.where(lane == 0, pltpu.roll(ghost_west, lax.rem(128 - r, 128), 1), pltpu.roll(x, 1, 1))
        res = wts[0, pl.ds(r, 1), :] * e + wts[1, pl.ds(r, 1), :] * w
        res = res + wts[2, pl.ds(r, 1), :] * field[r + 2]
        res = res + wts[3, pl.ds(r, 1), :] * field[r]
        return res - wts[4, pl.ds(r, 1), :] * x

    ghost_w = recv[2, 0:16]
    ghost_e = recv[3, 0:16]

    def feature_rows(i, carry):
        for k in range(4):
            r = i * 4 + k
            lap = lap_row(xt, ghost_w, ghost_e, r)
            feat[r] = jnp.concatenate([xt[r + 1], lap], axis=0).astype(BF16)
        return carry

    lax.fori_loop(0, rows // 8, feature_rows, 0)
    for copy in mom_lat_copies:
        copy.wait()
    part = mom[...]
    for d in range(1, nlat):
        part = part + mom_lat[d]
    mom_lon[0] = part
    mom_lon_copies = [
        remote(mom_lon.at[0], mom_lon.at[d], mo_send.at[d], mo_recv.at[d], {"lon": lon_peer(d)})
        for d in range(1, nlon)
    ]
    for copy in mom_lon_copies:
        copy.start()
    lax.fori_loop(rows // 8, rows // 4, feature_rows, 0)
    for copy in mom_lon_copies:
        copy.wait()
    part = mom_lon[0]
    for d in range(1, nlon):
        part = part + mom_lon[d]
    sums = jnp.sum(part, axis=1, keepdims=True)
    coefficients = krylov_coefficients([sums[k:k + 1, :] for k in range(6)])
    scale = 1.0 / math.sqrt(L)
    pres[...] = scale * (
        coefficients[0] * basis[0] + coefficients[1] * basis[1] + coefficients[2] * basis[2]
    )

    def closure(i, carry):
        low, high = carry
        adjoints, grads, feats = [], [], []
        for k in range(GROUP):
            r = i * GROUP + k
            live = level < wts[5, pl.ds(r, 1), :]
            adj = cot[pl.ds(r, L, stride=rows), :] + jnp.where(live, pres[pl.ds(r, 1), :], 0.0)
            adjoints.append(adj)
            grads.append(jnp.where(live, CLOSURE_STEP * adj, 0.0).astype(BF16))
            feats.append(feat[r])
        features = jnp.concatenate(feats, axis=1)
        grad = jnp.concatenate(grads, axis=1)
        bias_tile = jnp.concatenate([bias_b[...]] * GROUP, axis=1)
        act = jnp.tanh(jnp.dot(w_in_t[...], features, preferred_element_type=F32) + bias_tile)
        back = jnp.dot(w_out[...], grad, preferred_element_type=F32)
        pre = back * (1.0 - act * act)
        half = pre.astype(BF16)
        acc = pre[:, 0:128]
        for k in range(1, GROUP):
            acc = acc + pre[:, k * 128:(k + 1) * 128]
        bias_acc[...] += acc
        gi_acc[...] += dot_nt(features, half)
        go_acc[...] += dot_nt(grad, act.astype(BF16))
        fg = jnp.dot(w_in[...], half, preferred_element_type=F32)
        for k in range(GROUP):
            r = i * GROUP + k
            z = DIFFUSE * adjoints[k] + fg[16:32, k * 128:(k + 1) * 128]
            zt[r + 1] = z
            yt[r] = adjoints[k] + fg[0:16, k * 128:(k + 1) * 128]
            low = jnp.where(lane == r, z[:, 0:1], low)
            high = jnp.where(lane == r, z[:, 127:128], high)
        return low, high

    low, high = lax.fori_loop(0, rows // GROUP, closure, (zeros, zeros))

    zmsg[0] = zt[1]
    zmsg[1] = zt[rows]
    zmsg[2] = low
    zmsg[3] = high
    z_edges = edge_copies(zmsg, zrecv, z_send, z_recv)
    z_tops = top_copies(zmsg.at[1], ztop, zt_send, zt_recv)
    start_edges(z_edges, z_tops)

    share = TILES // nlat
    ones = jnp.full((8, 128), 1.0, F32)
    bias_rows = exact_dot(ones, bias_acc[...], (((1,), (1,)), ((), ())))
    for half_at in range(2):
        cols = slice(half_at * 128, half_at * 128 + 128)
        for t in range(4):
            gpart[half_at * 8 + t] = gi_acc[t * 8:t * 8 + 8, cols]
        for t in range(2):
            gpart[half_at * 8 + 4 + t] = go_acc[t * 8:t * 8 + 8, cols]
        gpart[half_at * 8 + 6] = bias_rows[:, cols]
        gpart[half_at * 8 + 7] = jnp.zeros((8, 128), F32)

    rs_copies = [
        remote(
            gpart.at[pl.ds(lat_peer(d) * share, share)], g_rs.at[d],
            rs_send.at[d], rs_recv.at[d], {"lat": lat_peer(d)},
        )
        for d in range(1, nlat)
    ]
    for copy in rs_copies:
        copy.start()
    for copy in rs_copies:
        copy.wait()
    mine = gpart[pl.ds(lat * share, share)]
    for d in range(1, nlat):
        mine = mine + g_rs[d]
    g_lon[0] = mine
    gl_copies = [
        remote(g_lon.at[0], g_lon.at[d], gl_send.at[d], gl_recv.at[d], {"lon": lon_peer(d)})
        for d in range(1, nlon)
    ]
    for copy in gl_copies:
        copy.start()

    finish_edges(z_edges, z_tops)

    @pl.when(has_south)
    def _():
        zt[0] = zrecv[0]

    @pl.when(jnp.logical_not(has_south))
    def _():
        zt[0] = zeros

    @pl.when(has_north)
    def _():
        zt[rows + 1] = zrecv[1]

    @pl.when(at_top)
    def _():
        folded = exact_dot(zmsg[1], fold_select(fold[...], lon, lon, 128, 192, size_lon))
        for d in range(1, nlon):
            block = lax.rem(lon + nlon - d, nlon)
            folded = folded + exact_dot(ztop[d], fold_select(fold[...], lon, block, 128, 192, size_lon))
        zt[rows + 1] = folded

    z_west = zrecv[2]
    z_east = zrecv[3]

    def final_rows(i, carry):
        for k in range(4):
            r = i * 4 + k
            out[pl.ds(r, L, stride=rows), :] = yt[r] + lap_row(zt, z_west, z_east, r)
        return carry

    lax.fori_loop(0, rows // 8, final_rows, 0)
    for copy in gl_copies:
        copy.wait()
    mine = g_lon[0]
    for d in range(1, nlon):
        mine = mine + g_lon[d]
    grad_scale = 1.0 / math.sqrt(rows * nlat * 128 * nlon)
    g_own[...] = mine * grad_scale
    g_full[pl.ds(lat * share, share)] = g_own[...]
    ag_copies = [
        remote(
            g_own, g_full.at[pl.ds(lat * share, share)],
            ag_send.at[d], ag_recv.at[d], {"lat": lat_peer(d)},
        )
        for d in range(1, nlat)
    ]
    for copy in ag_copies:
        copy.start()
    lax.fori_loop(rows // 8, rows // 4, final_rows, 0)
    for copy in ag_copies:
        copy.wait()
    for half_at in range(2):
        cols = slice(half_at * 128, half_at * 128 + 128)
        for t in range(4):
            g_in[t * 8:t * 8 + 8, cols] = g_full[half_at * 8 + t]
        block = jnp.concatenate(
            [g_full[half_at * 8 + 4], g_full[half_at * 8 + 5], jnp.zeros((112, 128), F32)], axis=0
        )
        g_out[half_at * 128:half_at * 128 + 128, :] = block.T[:, 0:16]
        g_bias[0:1, cols] = g_full[half_at * 8 + 6, 0:1, :]


def on_device(nlat, nlon, state, cotangent, land_mask, level_count, fold_partner, weight_in, weight_out, bias_hidden):
    rows, cols = land_mask.shape
    vm = pltpu.VMEM
    dma = pltpu.SemaphoreType.DMA
    share = TILES // nlat
    scratch = [
        vm((rows + 2, L, 128), F32), vm((rows + 2, L, 128), F32), vm((rows, L, 128), F32),
        vm((rows, 2 * L, 128), BF16), vm((rows + 16, 256), F32), vm((rows + 16, 256), F32),
        vm((6, rows, 128), F32), vm((3, rows, 128), F32), vm((rows, 128), F32),
        vm((H, 2 * L), BF16), vm((H, 128), F32), vm((H, 128), F32),
        vm((2 * L, H), F32), vm((L, H), F32),
        vm((4, 32, 128), F32), vm((4, 32, 128), F32), vm((4, 16, 128), F32), vm((nlon, 32, 128), F32),
        vm((4, L, 128), F32), vm((4, L, 128), F32), vm((nlon, L, 128), F32),
        vm((8, 128), F32), vm((nlat, 8, 128), F32), vm((nlon, 8, 128), F32),
        vm((TILES, 8, 128), F32), vm((nlat, share, 8, 128), F32), vm((share, 8, 128), F32),
        vm((nlon, share, 8, 128), F32), vm((TILES, 8, 128), F32),
        dma((4,)), dma((4,)), dma((4,)), dma((4,)), dma((nlon,)), dma((nlon,)),
        dma((nlat,)), dma((nlat,)), dma((nlon,)), dma((nlon,)),
        dma((4,)), dma((4,)), dma((nlon,)), dma((nlon,)),
        dma((nlat,)), dma((nlat,)), dma((nlon,)), dma((nlon,)), dma((nlat,)), dma((nlat,)),
    ]
    spec = pl.BlockSpec(memory_space=pltpu.VMEM)
    out, g_in, g_out, g_bias = pl.pallas_call(
        functools.partial(kernel, nlat, nlon),
        out_shape=(
            jax.ShapeDtypeStruct((L * rows, cols), F32),
            jax.ShapeDtypeStruct((2 * L, H), F32),
            jax.ShapeDtypeStruct((H, L), F32),
            jax.ShapeDtypeStruct((1, H), F32),
        ),
        in_specs=[spec] * 8,
        out_specs=(spec,) * 4,
        scratch_shapes=scratch,
        compiler_params=pltpu.CompilerParams(
            collective_id=0, has_side_effects=True, vmem_limit_bytes=40 * 1024 * 1024
        ),
    )(
        state.reshape(L * rows, cols), cotangent.reshape(L * rows, cols), land_mask, level_count,
        fold_partner.reshape(1, cols), weight_in, weight_out, bias_hidden.reshape(1, H),
    )
    return out.reshape(L, rows, cols), g_in, g_out, g_bias.reshape(H)


def solution(mesh):
    placed = (
        P("ens", "lat", "lon"), P("ens", "lat", "lon"), P("lat", "lon"), P("lat", "lon"),
        P("lon"), P(), P(), P(),
    )
    body = functools.partial(on_device, mesh.shape["lat"], mesh.shape["lon"])
    return jax.shard_map(
        body,
        mesh=mesh,
        in_specs=placed,
        out_specs=(P("ens", "lat", "lon"), P("ens", None), P("ens", None), P("ens")),
        check_vma=False,
    )
```

time: 478 us -> 54.7 us (0.11)
  blocking collectives: 269 us -> 0 us
  local copies, waits for them, and re-layouts: 78.8 us -> 7.69 us
  Pallas kernels: 0 us -> 45.9 us
  starting transfers between devices: 42.6 us -> 0 us
  other arithmetic: 32.1 us -> 0 us
  matrix products: 21.8 us -> 0 us
  waiting for transfers between devices: 11.6 us -> 0 us
  loops' own time: 11.4 us -> 0 us
  between operations: 7.79 us -> 0.7 us
    psum x6 -> x0, blocking collectives: 208 us -> none  [the longest x3 90.4 us: squares(): return lax.psum(jnp.sum(residual * residual), ('lon', 'lat'))]
    all_gather x6 -> x0, blocking collectives: 60.3 us -> none  [neighbours(): top_row = lax.all_gather(grid_field[:, -1, :], 'lon', axis=1, tiled=True)]
    pallas_call x0 -> x1, Pallas kernels: none -> 45.9 us  [on_device(): pl.pallas_call(functools.partial(kernel, nlat, nlon), out_shape=(jax.Shap...]
    ppermute x24 -> x0, starting transfers between devices: 42.6 us -> none  [the longest x12 23.4 us: with_halo(): lax.ppermute(lax.slice_in_dim(block, block.shape[dim] - width, None, axis...]
    dynamic_slice x48 -> x0, local copies, waits for them, and re-layouts: 35.2 us -> none  [the longest x16 13.5 us: one_block(): lax.dynamic_slice_in_dim(features, start, 8, 1)]
    dot_general x80 -> x0, matrix products: 21.8 us -> none  [the longest x16 6.35 us: one_block(): jnp.einsum('hl,ln->hn', weight_out, grad_block, preferred_element_type=jn...]
    slice x18 -> x0, local copies, waits for them, and re-layouts: 12.2 us -> none  [the longest x11 7.42 us: with_halo(): lax.slice_in_dim(block, 0, width, axis=dim)]
    ppermute x24 -> x0, waiting for transfers between devices: 11.6 us -> none  [the longest x12 9.4 us: with_halo(): lax.ppermute(lax.slice_in_dim(block, block.shape[dim] - width, None, axis...]
  transfers between devices with their start and end apart: 24 -> 0, of which waited for: 3 -> 0; matrix products, arithmetic and copies ran while one was open for 11% -> 0% of each run, Pallas kernels for 0% -> 0%
where the time goes in v1:
time: 54.7 us; the launch traced here: 54.3 us
  Pallas kernels  45.9 us (84%)
  local copies, waits for them, and re-layouts  7.69 us (14%)
  between operations  0.7 us (1%)
    pallas_call x1, Pallas kernels, on_device(): pl.pallas_call(functools.partial(kernel, nlat, nlon), out_shape=(jax.Shap...  45.9 us
    unnamed x19, local copies, waits for them, and re-layouts  7.69 us

profile of v1, /device:TPU:0, one launch (start us, length us, event | category | flops | bytes accessed | tf_op | source)
XLA Modules:
  0.0 54.3 jit_solution(4658329350091591338)
XLA Ops:
  0.6 0.0 copy-start.2
  0.6 0.0 copy-start.5
  0.7 0.0 copy-start.6
  0.7 0.8 %copy.12.w_out = bf16[256,16]{1,0:T(8,128)(2,1)S(1)} copy(bf16[256,16]{0,1:T(8,128)(2,1)} %param.14) | data formatting | bytes 16384 | tf_op args[6]
  1.5 0.0 copy-done.2
  1.5 0.0 copy-done.5
  1.5 0.0 copy-done.6
  1.5 0.0 copy-start
  1.5 1.2 %copy-done = f32[16,128,128]{2,1,0:T(8,128)S(1)} copy-done((f32[16,128,128]{2,1,0:T(8,128)S(1)}, f32[16,128,128]{2,1,0:T(8,128)}, u32[]{:S(2)}) %copy-start) | copy-done | bytes 1048600
  2.8 0.0 copy-start.1
  2.8 1.2 %copy-done.1 = f32[16,128,128]{2,1,0:T(8,128)S(1)} copy-done((f32[16,128,128]{2,1,0:T(8,128)S(1)}, f32[16,128,128]{2,1,0:T(8,128)}, u32[]{:S(2)}) %copy-start.1) | copy-done | bytes 1048600
  4.0 0.0 copy-start.3
  4.0 0.8 %copy-done.3 = s32[128,128]{1,0:T(8,128)S(1)} copy-done((s32[128,128]{1,0:T(8,128)S(1)}, s32[128,128]{1,0:T(8,128)}, u32[]{:S(2)}) %copy-start.3) | copy-done | bytes 65560
  4.8 0.0 copy-start.4
  4.8 0.7 %copy-done.4 = bf16[32,256]{1,0:T(8,128)(2,1)S(1)} copy-done((bf16[32,256]{1,0:T(8,128)(2,1)S(1)}, bf16[32,256]{1,0:T(8,128)(2,1)}, u32[]{:S(2)}) %copy-start.4) | copy-done | bytes 16408
  5.5 45.9 %shard_map.111 = (f32[2048,128]{1,0:T(8,128)S(1)}, f32[32,256]{1,0:T(8,128)S(1)}, f32[256,16]{1,0:T(8,128)S(1)}, f32[1,256]{1,0:T(1,128)S(1)}) custom-call(f32[2048,128]{1,0:T(8,128)S(1)} %bitcast.6, f32[2048,128]{1,0:T(8,128)S(1)} %bitcast.7, s32[128,128]{1,0:T(8,128)S(1)} %copy-done.2, s32[128,128]{1,0:T(8,128)S(1)} %copy-done.3, s32[1,128]{1,0:T(1,128)S(1)} %bitcast.11, ...), custom_call_target="tpu_custom_call" | custom-call | tf_op jit(solution)/shard_map/pallas_call | solution.py:581
  51.5 0.7 %copy.13 = f32[256,16]{0,1:T(8,128)} copy(f32[256,16]{1,0:T(8,128)S(1)} %get-tuple-element.14) | data formatting | bytes 32768
  52.2 1.0 %copy.17 = f32[16,128,128]{2,1,0:T(8,128)} copy(f32[16,128,128]{2,1,0:T(8,128)S(1)} %bitcast.8) | data formatting | bytes 2097152
  53.1 0.6 %copy.18 = f32[32,256]{1,0:T(8,128)} copy(f32[32,256]{1,0:T(8,128)S(1)} %get-tuple-element.21) | data formatting | bytes 65536
  53.8 0.6 %copy.19 = f32[256]{0:T(256)} copy(f32[256]{0:T(256)S(1)} %bitcast.10) | data formatting | bytes 2048
Async XLA Ops:
  0.6 0.9 %copy-start.2 = (s32[128,128]{1,0:T(8,128)S(1)}, s32[128,128]{1,0:T(8,128)}, u32[]{:S(2)}) copy-start(s32[128,128]{1,0:T(8,128)} %mask.1) | copy-start | bytes 196612
  0.6 0.9 %copy-start.5 = (f32[256]{0:T(256)S(1)}, f32[256]{0:T(256)}, u32[]{:S(2)}) copy-start(f32[256]{0:T(256)} %param.15) | copy-start | bytes 3076
  0.7 0.9 %copy-start.6 = (s32[128]{0:T(128)S(1)}, s32[128]{0:T(128)}, u32[]{:S(2)}) copy-start(s32[128]{0:T(128)} %param.12) | copy-start | bytes 1540
  1.5 1.2 %copy-start = (f32[16,128,128]{2,1,0:T(8,128)S(1)}, f32[16,128,128]{2,1,0:T(8,128)}, u32[]{:S(2)}) copy-start(f32[16,128,128]{2,1,0:T(8,128)} %param.8) | copy-start | bytes 3145732
  2.8 1.2 %copy-start.1 = (f32[16,128,128]{2,1,0:T(8,128)S(1)}, f32[16,128,128]{2,1,0:T(8,128)}, u32[]{:S(2)}) copy-start(f32[16,128,128]{2,1,0:T(8,128)} %param.9) | copy-start | bytes 3145732
  4.0 0.8 %copy-start.3 = (s32[128,128]{1,0:T(8,128)S(1)}, s32[128,128]{1,0:T(8,128)}, u32[]{:S(2)}) copy-start(s32[128,128]{1,0:T(8,128)} %count.1) | copy-start | bytes 196612
  4.8 0.7 %copy-start.4 = (bf16[32,256]{1,0:T(8,128)(2,1)S(1)}, bf16[32,256]{1,0:T(8,128)(2,1)}, u32[]{:S(2)}) copy-start(bf16[32,256]{1,0:T(8,128)(2,1)} %w_in.1) | copy-start | bytes 49156

commit v2 on v1

--- a/solution.py
+++ b/solution.py
@@ -19,7 +19,7 @@
 SHIFT = 4.25
 SPAN = 4.15
 TILES = 16
-GROUP = 4
+GROUP = 16
 
 
 def fold_select(fold, lon, block, width, east_lanes, size):
@@ -85,16 +85,17 @@
 
 def kernel(
     nlat, nlon,
-    state, cot, mask, count, fold, w_in, w_out, bias,
+    state_h, cot_h, mask_h, count_h, fold, w_in, w_out_t, bias,
     out, g_in, g_out, g_bias,
-    xt, zt, yt, feat, bext, cext, wts, basis, pres, w_in_t, bias_b, bias_acc,
+    state, cot, mask, count, load_sem,
+    xt, zt, yt, feat, bext, cext, wts, basis, pres, w_in_t, w_out_b, bias_b, bias_acc,
     gi_acc, go_acc,
     msg, recv, diag, top, zmsg, zrecv, ztop,
-    mom, mom_lat, mom_lon, gpart, g_rs, g_own, g_lon, g_full,
+    mom, mom_in, gpart, g_rs, g_own, g_full,
     e_send, e_recv, d_send, d_recv, t_send, t_recv,
-    ml_send, ml_recv, mo_send, mo_recv,
+    m_send, m_recv,
     z_send, z_recv, zt_send, zt_recv,
-    rs_send, rs_recv, gl_send, gl_recv, ag_send, ag_recv,
+    rs_send, rs_recv, ag_send, ag_recv,
 ):
     rows = mask.shape[0]
     size_lon = nlon * 128
@@ -108,31 +109,32 @@
     west = lax.rem(lon + nlon - 1, nlon)
     east = lax.rem(lon + 1, nlon)
 
-    def lat_peer(d):
-        return lax.rem(lat + d, nlat)
-
     def lon_peer(d):
         return lax.rem(lon + d, nlon)
 
+    group = nlat * nlon
+    me = lon * nlat + lat
+
+    def peer_index(d):
+        return lax.rem(me + d, group)
+
+    def peer(d):
+        index = peer_index(d)
+        return {"lat": lax.rem(index, nlat), "lon": index // nlat}
+
+    loads = [
+        pltpu.make_async_copy(source, target, load_sem.at[k])
+        for k, (source, target) in enumerate(
+            ((mask_h, mask), (count_h, count), (cot_h, cot), (state_h, state))
+        )
+    ]
+    for load in loads:
+        load.start()
     barrier = pltpu.get_barrier_semaphore()
-    for d in range(1, nlat):
-        pl.semaphore_signal(barrier, inc=1, device_id={"lat": lat_peer(d)}, device_id_type=MESH)
-    for d in range(1, nlon):
-        pl.semaphore_signal(barrier, inc=1, device_id={"lon": lon_peer(d)}, device_id_type=MESH)
-
-    @pl.when(has_south)
-    def _():
-        for side in (west, east):
-            pl.semaphore_signal(
-                barrier, inc=1, device_id={"lat": south, "lon": side}, device_id_type=MESH
-            )
-
-    @pl.when(has_north)
-    def _():
-        for side in (west, east):
-            pl.semaphore_signal(
-                barrier, inc=1, device_id={"lat": north, "lon": side}, device_id_type=MESH
-            )
+    for d in range(1, group):
+        pl.semaphore_signal(barrier, inc=1, device_id=peer(d), device_id_type=MESH)
+    for load in loads[:3]:
+        load.wait()
 
     mask_f = mask[...].astype(F32)
     live_count = mask_f * count[...].astype(F32)
@@ -159,6 +161,7 @@
         return low, high
 
     zeros = jnp.zeros((L, 128), F32)
+    loads[3].wait()
     low, high = lax.fori_loop(0, rows // 8, transpose_rows, (zeros, zeros))
 
     msg[0, 0:16] = xt[1]
@@ -174,8 +177,7 @@
     msg[3, 16:24] = right_t[120:128]
     msg[3, 24:32] = count_t[120:128]
 
-    waits = (nlat - 1) + (nlon - 1) + 2 * has_south.astype(jnp.int32) + 2 * has_north.astype(jnp.int32)
-    pl.semaphore_wait(barrier, waits)
+    pl.semaphore_wait(barrier, group - 1)
 
     def remote(src, dst, send, receive, device):
         return pltpu.make_async_remote_copy(
@@ -255,6 +257,9 @@
 
     pad = jnp.zeros((96, H), F32)
     w_in_t[...] = jnp.concatenate([w_in[...].astype(F32), pad], axis=0).T[:, 0:32].astype(BF16)
+    w_out_b[...] = jnp.concatenate(
+        [w_out_t[...].astype(F32), jnp.zeros((112, H), F32)], axis=0
+    ).T[:, 0:L].astype(BF16)
     bias_b[...] = jnp.broadcast_to(bias[...], (128, H)).T
     bias_acc[...] = jnp.zeros_like(bias_acc)
     gi_acc[...] = jnp.zeros_like(gi_acc)
@@ -364,11 +369,10 @@
          colsum(u2, u2), colsum(u2, u3), jnp.zeros((2, 128), F32)], axis=0
     )
 
-    mom_lat_copies = [
-        remote(mom, mom_lat.at[d], ml_send.at[d], ml_recv.at[d], {"lat": lat_peer(d)})
-        for d in range(1, nlat)
+    mom_copies = [
+        remote(mom, mom_in.at[d], m_send.at[d], m_recv.at[d], peer(d)) for d in range(1, group)
     ]
-    for copy in mom_lat_copies:
+    for copy in mom_copies:
         copy.start()
 
     def lap_row(field, ghost_west, ghost_east, r):
@@ -384,31 +388,19 @@
     ghost_e = recv[3, 0:16]
 
     def feature_rows(i, carry):
-        for k in range(4):
-            r = i * 4 + k
+        for k in range(16):
+            r = i * 16 + k
             lap = lap_row(xt, ghost_w, ghost_e, r)
-            feat[r] = jnp.concatenate([xt[r + 1], lap], axis=0).astype(BF16)
+            both = jnp.concatenate([xt[r + 1], lap], axis=0)
+            feat[r] = both.astype(BF16)
         return carry
 
-    lax.fori_loop(0, rows // 8, feature_rows, 0)
-    for copy in mom_lat_copies:
+    lax.fori_loop(0, rows // 16, feature_rows, 0)
+    for copy in mom_copies:
         copy.wait()
     part = mom[...]
-    for d in range(1, nlat):
-        part = part + mom_lat[d]
-    mom_lon[0] = part
-    mom_lon_copies = [
-        remote(mom_lon.at[0], mom_lon.at[d], mo_send.at[d], mo_recv.at[d], {"lon": lon_peer(d)})
-        for d in range(1, nlon)
-    ]
-    for copy in mom_lon_copies:
-        copy.start()
-    lax.fori_loop(rows // 8, rows // 4, feature_rows, 0)
-    for copy in mom_lon_copies:
-        copy.wait()
-    part = mom_lon[0]
-    for d in range(1, nlon):
-        part = part + mom_lon[d]
+    for d in range(1, group):
+        part = part + mom_in[d]
     sums = jnp.sum(part, axis=1, keepdims=True)
     coefficients = krylov_coefficients([sums[k:k + 1, :] for k in range(6)])
     scale = 1.0 / math.sqrt(L)
@@ -423,14 +415,15 @@
             r = i * GROUP + k
             live = level < wts[5, pl.ds(r, 1), :]
             adj = cot[pl.ds(r, L, stride=rows), :] + jnp.where(live, pres[pl.ds(r, 1), :], 0.0)
+            grad = jnp.where(live, CLOSURE_STEP * adj, 0.0)
             adjoints.append(adj)
-            grads.append(jnp.where(live, CLOSURE_STEP * adj, 0.0).astype(BF16))
+            grads.append(grad.astype(BF16))
             feats.append(feat[r])
         features = jnp.concatenate(feats, axis=1)
         grad = jnp.concatenate(grads, axis=1)
         bias_tile = jnp.concatenate([bias_b[...]] * GROUP, axis=1)
         act = jnp.tanh(jnp.dot(w_in_t[...], features, preferred_element_type=F32) + bias_tile)
-        back = jnp.dot(w_out[...], grad, preferred_element_type=F32)
+        back = jnp.dot(w_out_b[...], grad, preferred_element_type=F32)
         pre = back * (1.0 - act * act)
         half = pre.astype(BF16)
         acc = pre[:, 0:128]
@@ -459,9 +452,7 @@
     z_tops = top_copies(zmsg.at[1], ztop, zt_send, zt_recv)
     start_edges(z_edges, z_tops)
 
-    share = TILES // nlat
-    ones = jnp.full((8, 128), 1.0, F32)
-    bias_rows = exact_dot(ones, bias_acc[...], (((1,), (1,)), ((), ())))
+    bias_rows = exact_dot(jnp.full((8, 128), 1.0, F32), bias_acc[...], (((1,), (1,)), ((), ())))
     for half_at in range(2):
         cols = slice(half_at * 128, half_at * 128 + 128)
         for t in range(4):
@@ -471,27 +462,43 @@
         gpart[half_at * 8 + 6] = bias_rows[:, cols]
         gpart[half_at * 8 + 7] = jnp.zeros((8, 128), F32)
 
+    owner = me < TILES
+    my_tile = lax.rem(me, TILES)
     rs_copies = [
         remote(
-            gpart.at[pl.ds(lat_peer(d) * share, share)], g_rs.at[d],
-            rs_send.at[d], rs_recv.at[d], {"lat": lat_peer(d)},
+            gpart.at[lax.rem(peer_index(d), TILES)], g_rs.at[d],
+            rs_send.at[d], rs_recv.at[d], peer(d),
         )
-        for d in range(1, nlat)
+        for d in range(1, group)
     ]
-    for copy in rs_copies:
-        copy.start()
-    for copy in rs_copies:
-        copy.wait()
-    mine = gpart[pl.ds(lat * share, share)]
-    for d in range(1, nlat):
-        mine = mine + g_rs[d]
-    g_lon[0] = mine
-    gl_copies = [
-        remote(g_lon.at[0], g_lon.at[d], gl_send.at[d], gl_recv.at[d], {"lon": lon_peer(d)})
-        for d in range(1, nlon)
+    ag_copies = [
+        remote(g_own, g_full.at[my_tile], ag_send.at[d], ag_recv.at[d], peer(d))
+        for d in range(1, group)
     ]
-    for copy in gl_copies:
-        copy.start()
+    all_own = group <= TILES
+
+    def guarded(condition, action):
+        if all_own:
+            action()
+        else:
+            pl.when(condition)(action)
+
+    for d, copy in enumerate(rs_copies, 1):
+        guarded(peer_index(d) < TILES, copy.start)
+    for d, copy in enumerate(rs_copies, 1):
+        guarded(peer_index(d) < TILES, copy.wait_send)
+        guarded(owner, copy.wait_recv)
+
+    def share_tile():
+        mine = gpart[my_tile]
+        for d in range(1, group):
+            mine = mine + g_rs[d]
+        g_own[...] = mine * (1.0 / math.sqrt(rows * nlat * 128 * nlon))
+        g_full[my_tile] = g_own[...]
+        for copy in ag_copies:
+            copy.start()
+
+    guarded(owner, share_tile)
 
     finish_edges(z_edges, z_tops)
 
@@ -519,84 +526,70 @@
     z_east = zrecv[3]
 
     def final_rows(i, carry):
-        for k in range(4):
-            r = i * 4 + k
+        for k in range(16):
+            r = i * 16 + k
             out[pl.ds(r, L, stride=rows), :] = yt[r] + lap_row(zt, z_west, z_east, r)
         return carry
 
-    lax.fori_loop(0, rows // 8, final_rows, 0)
-    for copy in gl_copies:
-        copy.wait()
-    mine = g_lon[0]
-    for d in range(1, nlon):
-        mine = mine + g_lon[d]
-    grad_scale = 1.0 / math.sqrt(rows * nlat * 128 * nlon)
-    g_own[...] = mine * grad_scale
-    g_full[pl.ds(lat * share, share)] = g_own[...]
-    ag_copies = [
-        remote(
-            g_own, g_full.at[pl.ds(lat * share, share)],
-            ag_send.at[d], ag_recv.at[d], {"lat": lat_peer(d)},
-        )
-        for d in range(1, nlat)
-    ]
-    for copy in ag_copies:
-        copy.start()
-    lax.fori_loop(rows // 8, rows // 4, final_rows, 0)
-    for copy in ag_copies:
-        copy.wait()
+    lax.fori_loop(0, rows // 16, final_rows, 0)
+    for d, copy in enumerate(ag_copies, 1):
+        guarded(owner, copy.wait_send)
+        guarded(lax.rem(me + group - d, group) < TILES, copy.wait_recv)
     for half_at in range(2):
         cols = slice(half_at * 128, half_at * 128 + 128)
         for t in range(4):
             g_in[t * 8:t * 8 + 8, cols] = g_full[half_at * 8 + t]
-        block = jnp.concatenate(
-            [g_full[half_at * 8 + 4], g_full[half_at * 8 + 5], jnp.zeros((112, 128), F32)], axis=0
-        )
-        g_out[half_at * 128:half_at * 128 + 128, :] = block.T[:, 0:16]
+        for t in range(2):
+            g_out[t * 8:t * 8 + 8, cols] = g_full[half_at * 8 + 4 + t]
         g_bias[0:1, cols] = g_full[half_at * 8 + 6, 0:1, :]
 
 
 def on_device(nlat, nlon, state, cotangent, land_mask, level_count, fold_partner, weight_in, weight_out, bias_hidden):
     rows, cols = land_mask.shape
+    group = nlat * nlon
     vm = pltpu.VMEM
     dma = pltpu.SemaphoreType.DMA
-    share = TILES // nlat
     scratch = [
+        vm((L * rows, 128), F32), vm((L * rows, 128), F32),
+        vm((rows, 128), jnp.int32), vm((rows, 128), jnp.int32), dma((4,)),
         vm((rows + 2, L, 128), F32), vm((rows + 2, L, 128), F32), vm((rows, L, 128), F32),
-        vm((rows, 2 * L, 128), BF16), vm((rows + 16, 256), F32), vm((rows + 16, 256), F32),
+        vm((rows, 2 * L, 128), BF16),
+        vm((rows + 16, 256), F32), vm((rows + 16, 256), F32),
         vm((6, rows, 128), F32), vm((3, rows, 128), F32), vm((rows, 128), F32),
-        vm((H, 2 * L), BF16), vm((H, 128), F32), vm((H, 128), F32),
+        vm((H, 2 * L), BF16), vm((H, L), BF16), vm((H, 128), F32), vm((H, 128), F32),
         vm((2 * L, H), F32), vm((L, H), F32),
         vm((4, 32, 128), F32), vm((4, 32, 128), F32), vm((4, 16, 128), F32), vm((nlon, 32, 128), F32),
         vm((4, L, 128), F32), vm((4, L, 128), F32), vm((nlon, L, 128), F32),
-        vm((8, 128), F32), vm((nlat, 8, 128), F32), vm((nlon, 8, 128), F32),
-        vm((TILES, 8, 128), F32), vm((nlat, share, 8, 128), F32), vm((share, 8, 128), F32),
-        vm((nlon, share, 8, 128), F32), vm((TILES, 8, 128), F32),
+        vm((8, 128), F32), vm((group, 8, 128), F32),
+        vm((TILES, 8, 128), F32), vm((group, 8, 128), F32), vm((8, 128), F32),
+        vm((TILES, 8, 128), F32),
         dma((4,)), dma((4,)), dma((4,)), dma((4,)), dma((nlon,)), dma((nlon,)),
-        dma((nlat,)), dma((nlat,)), dma((nlon,)), dma((nlon,)),
+        dma((group,)), dma((group,)),
         dma((4,)), dma((4,)), dma((nlon,)), dma((nlon,)),
-        dma((nlat,)), dma((nlat,)), dma((nlon,)), dma((nlon,)), dma((nlat,)), dma((nlat,)),
+        dma((group,)), dma((group,)), dma((group,)), dma((group,)),
     ]
     spec = pl.BlockSpec(memory_space=pltpu.VMEM)
+    hbm = pl.BlockSpec(memory_space=pltpu.HBM)
+    shapes = (
+        jax.ShapeDtypeStruct((L * rows, cols), F32),
+        jax.ShapeDtypeStruct((2 * L, H), F32),
+        jax.ShapeDtypeStruct((L, H), F32),
+        jax.ShapeDtypeStruct((1, H), F32),
+    )
     out, g_in, g_out, g_bias = pl.pallas_call(
         functools.partial(kernel, nlat, nlon),
-        out_shape=(
-            jax.ShapeDtypeStruct((L * rows, cols), F32),
-            jax.ShapeDtypeStruct((2 * L, H), F32),
-            jax.ShapeDtypeStruct((H, L), F32),
-            jax.ShapeDtypeStruct((1, H), F32),
-        ),
-        in_specs=[spec] * 8,
+        out_shape=shapes,
+        in_specs=[hbm] * 4 + [spec] * 4,
         out_specs=(spec,) * 4,
         scratch_shapes=scratch,
         compiler_params=pltpu.CompilerParams(
-            collective_id=0, has_side_effects=True, vmem_limit_bytes=40 * 1024 * 1024
+            collective_id=0, has_side_effects=True, vmem_limit_bytes=60 * 1024 * 1024
         ),
     )(
         state.reshape(L * rows, cols), cotangent.reshape(L * rows, cols), land_mask, level_count,
-        fold_partner.reshape(1, cols), weight_in, weight_out, bias_hidden.reshape(1, H),
-    )
-    return out.reshape(L, rows, cols), g_in, g_out, g_bias.reshape(H)
+        fold_partner.reshape(1, cols), weight_in, weight_out.T, bias_hidden.reshape(1, H),
+    )
+    return out.reshape(L, rows, cols), g_in, g_out.T, g_bias.reshape(H)
 
 
 def solution(mesh):

time: 54.7 us -> 45.2 us (0.83)
  Pallas kernels: 45.9 us -> 39.9 us
  local copies, waits for them, and re-layouts: 7.69 us -> 4.26 us
    pallas_call x1, Pallas kernels: 45.9 us -> 39.9 us  [on_device(): pl.pallas_call(functools.partial(kernel, nlat, nlon), out_shape=shapes, i...]
    unnamed x19 -> x10, local copies, waits for them, and re-layouts: 7.69 us -> 4.26 us
where the time goes in v2:
time: 45.2 us; the launch traced here: 44.8 us
  Pallas kernels  39.9 us (88%)
  local copies, waits for them, and re-layouts  4.26 us (9%)
  between operations  0.65 us (1%)
    pallas_call x1, Pallas kernels, on_device(): pl.pallas_call(functools.partial(kernel, nlat, nlon), out_shape=shapes, i...  39.9 us
    unnamed x10, local copies, waits for them, and re-layouts  4.26 us

profile of v2, /device:TPU:0, one launch (start us, length us, event | category | flops | bytes accessed | tf_op | source)
XLA Modules:
  0.0 44.8 jit_solution(11624701222911918614)
XLA Ops:
  0.6 39.9 %shard_map.111 = (f32[2048,128]{1,0:T(8,128)}, f32[32,256]{1,0:T(8,128)}, f32[16,256]{1,0:T(8,128)}, f32[1,256]{1,0:T(1,128)}) custom-call(f32[2048,128]{1,0:T(8,128)} %bitcast.8, f32[2048,128]{1,0:T(8,128)} %bitcast.9, s32[128,128]{1,0:T(8,128)} %mask_h.1, s32[128,128]{1,0:T(8,128)} %count_h.1, s32[1,128]{1,0:T(1,128)} %bitcast.15, bf16[32,256]{1,0:T(8,128)(2,1)} %w_in.1, ...), custom_call_target="tpu_custom_call" | custom-call | tf_op jit(solution)/shard_map/pallas_call | solution.py:579
  40.6 0.0 copy-start
  40.6 2.3 %copy.16 = f32[16,128,128]{2,1,0:T(8,128)} copy(f32[16,128,128]{2,1,0:T(8,128)} %bitcast.10) | data formatting | bytes 2097152
  42.9 0.0 copy-done
  42.9 0.0 copy-start.1
  42.9 0.6 %copy.17 = f32[32,256]{1,0:T(8,128)} copy(f32[32,256]{1,0:T(8,128)S(1)} %copy-done) | data formatting | bytes 65536
  43.5 0.1 copy-done.1
  43.6 0.0 copy-start.2
  43.6 0.6 %copy.18 = f32[256,16]{0,1:T(8,128)} copy(f32[256,16]{0,1:T(8,128)S(1)} %bitcast.11) | data formatting | bytes 32768
  44.2 0.1 copy-done.2
  44.3 0.6 %copy.19 = f32[256]{0:T(256)} copy(f32[256]{0:T(256)S(1)} %bitcast.14) | data formatting | bytes 2048
Async XLA Ops:
  40.6 2.3 %copy-start = (f32[32,256]{1,0:T(8,128)S(1)}, f32[32,256]{1,0:T(8,128)}, u32[]{:S(2)}) copy-start(f32[32,256]{1,0:T(8,128)} %get-tuple-element.17) | copy-start | bytes 98308
  42.9 0.7 %copy-start.1 = (f32[16,256]{1,0:T(8,128)S(1)}, f32[16,256]{1,0:T(8,128)}, u32[]{:S(2)}) copy-start(f32[16,256]{1,0:T(8,128)} %get-tuple-element.10) | copy-start | bytes 49156
  43.6 0.7 %copy-start.2 = (f32[1,256]{1,0:T(1,128)S(1)}, f32[1,256]{1,0:T(1,128)}, u32[]{:S(2)}) copy-start(f32[1,256]{1,0:T(1,128)} %get-tuple-element.11) | copy-start | bytes 3076
